TPU v7x, 32 devices: a whole 2x2x4 slice. The times are simulated.
32 devices in a mesh: row: 8 (over y, x, core), col: 4 (over z).
Axes of the slice: x: 2, y: 2, z: 4, core: 2. Of those that a mesh axis runs over, the one named last changes fastest.
Arguments:
- amplitudes: bfloat16 [6144, 6144], P('row', 'col'), may hold values from -6 to 6
- integrals: bfloat16 [6144, 6144], P('row', 'col'), may hold values from -0.078125 to 0.078125
- dressing: bfloat16 [6144, 3072], P(None, 'col'), may hold values from -0.078125 to 0.078125
Outputs:
- first_cycle: float32 [6144, 6144], P('row', 'col')
- second_cycle: float32 [6144, 3072], P('row', 'col')
All inputs are finite; a program needn't handle non-finite values.
Results may differ from a plain program's by a relative error of at most 0.0029.
Values may be sent and summed in bfloat16 or wider, within the bound.
A program may use at most 128 MiB of HBM per device.

v0:
```python
import jax
import jax.numpy as jnp
from jax import lax
from jax.sharding import PartitionSpec as P


def per_device(amplitudes, integrals, dressing):
    amp_rows = lax.all_gather(amplitudes, "col", axis=1, tiled=True)
    first_cycle = jnp.dot(
        amp_rows,
        lax.all_gather(integrals, "row", axis=0, tiled=True),
        preferred_element_type=jnp.float32,
    )
    rounded = first_cycle.astype(jnp.bfloat16)
    row_count = rounded.shape[0]
    own_rows = lax.dynamic_slice_in_dim(dressing, lax.axis_index("row") * row_count, row_count, 0)
    wide_rows = lax.all_gather(own_rows, "col", axis=1, tiled=True)
    summed = lax.psum_scatter(
        lax.dot_general(
            rounded, wide_rows, (((0,), (0,)), ((), ())), preferred_element_type=jnp.float32
        ),
        "row",
        scatter_dimension=0,
        tiled=True,
    )
    second_cycle = lax.all_to_all(summed, "col", split_axis=1, concat_axis=0, tiled=True)
    return (first_cycle, second_cycle)


def solution(mesh):
    placed = (P("row", "col"), P("row", "col"), P(None, "col"))
    return jax.shard_map(
        per_device,
        mesh=mesh,
        in_specs=placed,
        out_specs=(P("row", "col"), P("row", "col")),
        check_vma=False,
    )
```

profile of v0, /device:TPU:0, one launch (start us, length us, event | category | flops | bytes accessed | tf_op | source)
XLA Modules:
  0.0 576.7 jit_solution(14850142240159565014)
XLA Ops:
  7.2 0.0 all-gather.4.cloned.1.call-start
  7.2 0.7 all-gather.4.cloned.1.call-update
  7.9 0.0 all-gather.6.cloned.1.call-start
  7.9 0.7 all-gather.6.cloned.1.call-update
  8.6 0.0 all-gather.8.cloned.1.call-start
  8.7 2.4 constant_dynamic-slice_fusion
  11.1 0.0 all-gather.8.cloned.1.call-update
  11.1 0.0 reduce-scatter.2.cloned.1.call-start
  11.1 167.9 %all-gather.4.cloned.1.call-done = bf16[768,6144]{1,0:T(8,128)(2,1)} async-done(((bf16[768,1536]{1,0:T(8,128)(2,1)}), bf16[768,6144]{1,0:T(8,128)(2,1)}) %all-gather.4.cloned.1.call-update) | async-done | bytes 9437200 | tf_op jit(solution)/shard_map/all_gather | solution.py:8
  179.1 98.8 %all-gather.6.cloned.1.call-done = bf16[6144,1536]{1,0:T(8,128)(2,1)} async-done(((bf16[768,1536]{1,0:T(8,128)(2,1)}), bf16[6144,1536]{1,0:T(8,128)(2,1)}) %all-gather.6.cloned.1.call-update) | async-done | bytes 18874384 | tf_op jit(solution)/shard_map/all_gather | solution.py:11
  277.9 21.0 %fusion.2 = f32[768,1536]{1,0:T(8,128)} fusion(bf16[768,6144]{1,0:T(8,128)(2,1)} %all-gather.4.cloned.1.call-done, bf16[6144,1536]{1,0:T(8,128)(2,1)} %all-gather.6.cloned.1.call-done), kind=kOutput, calls=%fused_computation.4 | convolution fusion | flops 14495514624 | bytes 33030144 | tf_op jit(solution)/shard_map/dot_general | solution.py:9
  299.0 70.5 %all-gather.8.cloned.1.call-done = bf16[768,3072]{1,0:T(8,128)(2,1)} async-done(((bf16[768,768]{1,0:T(8,128)(2,1)}), bf16[768,3072]{1,0:T(8,128)(2,1)}) %all-gather.8.cloned.1.call-update) | async-done | bytes 4718608 | tf_op jit(solution)/shard_map/all_gather | solution.py:17
  369.5 14.5 %fusion = f32[1536,3072]{1,0:T(8,128)} fusion(bf16[768,3072]{1,0:T(8,128)(2,1)} %all-gather.8.cloned.1.call-done, f32[768,1536]{1,0:T(8,128)} %fusion.2), kind=kOutput, calls=%fused_computation.1 | convolution fusion | flops 7248936960 | bytes 28311552 | tf_op jit(solution)/shard_map/dot_general | solution.py:19
  384.0 0.0 reduce-scatter.2.cloned.1.call-update
  384.0 124.7 %reduce-scatter.2.cloned.1.call-done = f32[192,3072]{1,0:T(8,128)} async-done(((f32[1536,3072]{1,0:T(8,128)}), f32[192,3072]{1,0:T(8,128)}) %reduce-scatter.2.cloned.1.call-update) | async-done | bytes 2359312 | tf_op jit(solution)/shard_map/reduce_scatter | solution.py:18
  508.7 1.8 copy.9
  510.6 58.2 %all_to_all.19 = f32[192,4,768]{2,0,1:T(8,128)S(1)} all-to-all(f32[192,4,768]{2,0,1:T(8,128)S(1)} %bitcast.10), channel_id=1, replica_groups=mesh['row'=8,'col'=4] {'col'}, dimensions={1} | all-to-all | bytes 4718592 | tf_op jit(solution)/shard_map/all_to_all | solution.py:26
  568.8 1.4 copy.11
Async XLA Ops:
  7.2 171.9 %all-gather.4.cloned.1.call-start = ((), (), s32[]{:S(2)}) async-start(), calls=%async_computation.2 | async-start | bytes 11796480 | tf_op jit(solution)/shard_map/all_gather | solution.py:8
  7.9 270.0 %all-gather.6.cloned.1.call-start = ((), (), s32[]{:S(2)}) async-start(), calls=%async_computation.3 | async-start | bytes 21233664 | tf_op jit(solution)/shard_map/all_gather | solution.py:11
  8.6 360.9 %all-gather.8.cloned.1.call-start = ((), (), s32[]{:S(2)}) async-start(), calls=%async_computation.4 | async-start | bytes 5898240 | tf_op jit(solution)/shard_map/all_gather | solution.py:17
  11.1 497.7 %reduce-scatter.2.cloned.1.call-start = ((), (), s32[]{:S(2)}) async-start(), calls=%async_computation.5 | async-start | bytes 21233664 | tf_op jit(solution)/shard_map/reduce_scatter | solution.py:18
Sparse Core Ops, SparseCore 0:
  9.6 169.4 all-gather.3
  181.0 96.9 all-gather.5
  280.1 89.3 all-gather.7
  384.2 124.5 reduce-scatter.1
where the time goes:
time: 577 us
  waiting for transfers between devices  463 us (80%)
  blocking collectives  58.2 us (10%)
  matrix products  35.6 us (6%)
  between operations  13.8 us (2%)
    all_gather x1, waiting for transfers between devices, per_device(): amp_rows = lax.all_gather(amplitudes, 'col', axis=1, tiled=True)  168 us
    reduce_scatter x1, waiting for transfers between devices, per_device(): lax.psum_scatter(lax.dot_general(rounded, wide_rows, (((0,), (0,)), ((),...  125 us
    all_gather x1, waiting for transfers between devices, per_device(): lax.all_gather(integrals, 'row', axis=0, tiled=True)  98.8 us
    all_gather x1, waiting for transfers between devices, per_device(): wide_rows = lax.all_gather(own_rows, 'col', axis=1, tiled=True)  70.5 us
    all_to_all x1, blocking collectives, per_device(): lax.all_to_all(summed, 'col', split_axis=1, concat_axis=0, tiled=True)  58.2 us
    dot_general x1, matrix products, per_device(): jnp.dot(amp_rows, lax.all_gather(integrals, 'row', axis=0, tiled=True), p...  21 us
    dot_general x1, matrix products, per_device(): lax.dot_general(rounded, wide_rows, (((0,), (0,)), ((), ())), preferred_e...  14.5 us
  transfers between devices with their start and end apart: 4, of which 4 were waited for; matrix products, arithmetic and copies ran while one was open for 4% of the time, Pallas kernels for 0%

commit v1 on v0

v1 whole, which is shorter than its diff:
```python
import functools

import jax
import jax.numpy as jnp
from jax import lax
from jax.experimental import pallas as pl
from jax.experimental.pallas import tpu as pltpu
from jax.sharding import PartitionSpec as P

MESH = pl.DeviceIdType.MESH
F32 = jnp.float32


def tile_of(size, largest):
    return max(t for t in range(128, largest + 1, 128) if size % t == 0)


def kernel(
    n_row, n_col, part,
    a_ref, b_ref, d_ref, c_ref, out_ref,
    abuf, bbuf, dbuf, acc, turned, mine, chipsum, others,
    a_send, a_recv, d_send, d_recv, b_send, b_recv, s_send, s_recv,
    x_send, x_recv, r_send, r_recv, o_send, o_recv, local,
):
    n_chip = n_row // 2
    r, q = lax.axis_index("row"), lax.axis_index("col")
    core, chip = lax.rem(r, 2), lax.div(r, 2)
    sibling = r + 1 - 2 * core
    a_rows, depth = a_ref.shape
    b_rows, width = b_ref.shape
    d_cols = d_ref.shape[1]

    def peer(dist):
        return lax.rem(chip + dist, n_chip) * 2 + core

    def order(i):
        room = jnp.minimum(q, n_col - 1 - q)
        half = lax.div(i + 1, 2)
        near = jnp.where(lax.rem(i, 2) == 1, q - half, q + half)
        far = jnp.where(q <= n_col - 1 - q, i, n_col - 1 - i)
        return jnp.where(i <= 2 * room, near, far)

    def remote(src, dst, send, recv, where):
        return pltpu.make_async_remote_copy(
            src_ref=src, dst_ref=dst, send_sem=send, recv_sem=recv, device_id=where, device_id_type=MESH
        )

    barrier = pltpu.get_barrier_semaphore()
    partners = [{"row": peer(k)} for k in range(1, n_chip)] + [{"row": sibling}]
    partners += [{"col": lax.rem(q + k, n_col)} for k in range(1, n_col)]
    for where in partners:
        pl.semaphore_signal(barrier, inc=1, device_id=where, device_id_type=MESH)
    pl.semaphore_wait(barrier, len(partners))

    def b_slot(owner):
        return bbuf.at[pl.ds(pl.multiple_of(owner * b_rows, b_rows), b_rows), :]

    def b_copy(k):
        return remote(b_ref, b_slot(r), b_send.at[k], b_recv.at[k], {"row": peer(k)})

    def b_arrival(k):
        slot = b_slot(peer(n_chip - k))
        return remote(slot, slot, b_send.at[k], b_recv.at[k], {"row": peer(k)})

    def s_copy(k):
        slot = b_slot(peer(n_chip - k))
        src = b_ref if k == 0 else slot
        return remote(src, slot, s_send.at[k], s_recv.at[k], {"row": sibling})

    def s_arrival(k):
        slot = b_slot(lax.rem(chip + n_chip - k, n_chip) * 2 + 1 - core)
        return remote(slot, slot, s_send.at[k], s_recv.at[k], {"row": sibling})

    own_d = d_ref.at[pl.ds(pl.multiple_of(r * a_rows, a_rows), a_rows), :]

    def line_copy(own, buf, send, recv, z, side, is_own):
        src = own if is_own else buf.at[z]
        return remote(src, buf.at[z], send.at[z, side], recv.at[z], {"col": q - 1 + 2 * side})

    def line_start(own, buf, send, recv):
        @pl.when(q > 0)
        def _():
            line_copy(own, buf, send, recv, q, 0, True).start()

        @pl.when(q < n_col - 1)
        def _():
            line_copy(own, buf, send, recv, q, 1, True).start()

    def line_forward(own, buf, send, recv, z):
        side = jnp.where(z < q, 0, 1)
        line_copy(own, buf, send, recv, z, side, False).wait_recv()

        @pl.when((z < q) & (q < n_col - 1))
        def _():
            line_copy(own, buf, send, recv, z, 1, False).start()

        @pl.when((z > q) & (q > 0))
        def _():
            line_copy(own, buf, send, recv, z, 0, False).start()

    def line_drain(own, buf, send, recv):
        @pl.loop(0, n_col)
        def _(z):
            @pl.when((z <= q) & (q < n_col - 1))
            def _():
                line_copy(own, buf, send, recv, z, 1, False).wait_send()

            @pl.when((z >= q) & (q > 0))
            def _():
                line_copy(own, buf, send, recv, z, 0, False).wait_send()

    a_line = (a_ref, abuf, a_send, a_recv)
    d_line = (own_d, dbuf, d_send, d_recv)

    line_start(*a_line)
    for k in range(1, n_chip):
        b_copy(k).start()
    s_copy(0).start()
    loads = [
        pltpu.make_async_copy(a_ref, abuf.at[q], local.at[0]),
        pltpu.make_async_copy(b_ref, b_slot(r), local.at[1]),
        pltpu.make_async_copy(own_d, dbuf.at[q], local.at[2]),
    ]
    for load in loads:
        load.start()
    for load in loads:
        load.wait()

    middle = n_col // 2 + 1

    @pl.loop(1, middle)
    def _(i):
        line_forward(*a_line, order(i))

    line_start(*d_line)
    for k in range(1, n_chip):
        b_arrival(k).wait_recv()
        s_copy(k).start()

    def multiply(z):
        tile = tile_of(width, 256)

        @pl.loop(0, width // tile)
        def _(j):
            cols = pl.ds(pl.multiple_of(j * tile, tile), tile)
            rows = pl.ds(pl.multiple_of(z * depth, depth), depth)
            acc[:, cols] += jnp.dot(abuf[z], bbuf[rows, cols], preferred_element_type=F32)

    acc[...] = jnp.zeros_like(acc)
    for k in range(n_chip):
        s_arrival(k).wait_recv()

    @pl.loop(0, n_col)
    def _(i):
        @pl.when(i >= middle)
        def _():
            line_forward(*a_line, order(i))

        multiply(order(i))

    first_out = pltpu.make_async_copy(acc, c_ref, local.at[3])
    first_out.start()
    turn = tile_of(width, 256)

    @pl.loop(0, width // turn)
    def _(j):
        at = pl.ds(pl.multiple_of(j * turn, turn), turn)
        turned[at, :] = acc[:, at].T.astype(turned.dtype)

    def x_copy(z):
        return remote(mine.at[1 - core], chipsum.at[z], x_send.at[z], x_recv.at[z], {"row": sibling})

    def r_copy(z, k):
        target = lax.rem(chip + k, n_chip)
        return remote(
            chipsum.at[z, target], others.at[z, k - 1], r_send.at[z, k], r_recv.at[z, k], {"row": peer(k)}
        )

    def o_copy(z, sem):
        place = out_ref.at[pl.ds(pl.multiple_of(q * part, part), part), :]
        return remote(chipsum.at[z, chip], place, o_send.at[z], o_recv.at[sem], {"col": z})

    def o_arrival(z):
        place = out_ref.at[pl.ds(pl.multiple_of(z * part, part), part), :]
        return remote(place, place, o_send.at[z], o_recv.at[z], {"col": z})

    def o_own():
        place = out_ref.at[pl.ds(pl.multiple_of(q * part, part), part), :]
        return pltpu.make_async_copy(chipsum.at[q, chip], place, local.at[4])

    def finish(z):
        for k in range(1, n_chip):
            r_copy(z, k).wait_recv()
        total = chipsum[z, chip]
        for k in range(1, n_chip):
            total += others[z, k - 1]
        chipsum[z, chip] = total

        @pl.when(z == q)
        def _():
            o_own().start()

        @pl.when(z != q)
        def _():
            o_copy(z, q).start()

    @pl.loop(0, n_col)
    def _(i):
        z = order(i)

        @pl.when(i > 0)
        def _():
            line_forward(*d_line, z)
            x_copy(order(i - 1)).wait_send()

        tile = tile_of(d_cols, 256)

        @pl.loop(0, d_cols // tile)
        def _(j):
            cols = pl.ds(pl.multiple_of(j * tile, tile), tile)
            product = jnp.dot(turned[...], dbuf[z, :, cols], preferred_element_type=F32)
            for owner in range(n_row):
                mine[owner % 2, owner // 2, :, cols] = product[owner * part : (owner + 1) * part]

        x_copy(z).start()

        @pl.when(i > 0)
        def _():
            finish(order(i - 1))

        x_copy(z).wait_recv()
        for k in range(n_chip):
            chipsum[z, k] += mine[core, k]
        for k in range(1, n_chip):
            r_copy(z, k).start()

    last = order(jnp.int32(n_col - 1))
    finish(last)

    x_copy(last).wait_send()
    line_drain(*a_line)
    line_drain(*d_line)
    for k in range(1, n_chip):
        b_copy(k).wait_send()
    for k in range(n_chip):
        s_copy(k).wait_send()

    @pl.loop(0, n_col)
    def _(z):
        for k in range(1, n_chip):
            r_copy(z, k).wait_send()

        @pl.when(z != q)
        def _():
            o_copy(z, q).wait_send()
            o_arrival(z).wait_recv()

    o_own().wait()
    first_out.wait()


def per_device(n_row, n_col, amplitudes, integrals, dressing):
    rows, depth = amplitudes.shape
    width, d_cols = integrals.shape[1], dressing.shape[1]
    part, n_chip = width // n_row, n_row // 2
    bf16 = amplitudes.dtype
    dma = pltpu.SemaphoreType.DMA
    anywhere = pl.BlockSpec(memory_space=pl.ANY)
    total = depth * n_col
    return tuple(
        pl.pallas_call(
            functools.partial(kernel, n_row, n_col, part),
            out_shape=[
                jax.ShapeDtypeStruct((rows, width), F32),
                jax.ShapeDtypeStruct((part * n_col, d_cols), F32),
            ],
            in_specs=[anywhere] * 3,
            out_specs=[anywhere] * 2,
            scratch_shapes=[
                pltpu.VMEM((n_col, rows, depth), bf16),
                pltpu.VMEM((total, width), bf16),
                pltpu.VMEM((n_col, rows, d_cols), bf16),
                pltpu.VMEM((rows, width), F32),
                pltpu.VMEM((width, rows), bf16),
                pltpu.VMEM((2, n_chip, part, d_cols), F32),
                pltpu.VMEM((n_col, n_chip, part, d_cols), F32),
                pltpu.VMEM((n_col, n_chip - 1, part, d_cols), F32),
                dma((n_col, 2)), dma((n_col,)), dma((n_col, 2)), dma((n_col,)),
                dma((n_chip,)), dma((n_chip,)), dma((n_chip,)), dma((n_chip,)),
                dma((n_col,)), dma((n_col,)),
                dma((n_col, n_chip)), dma((n_col, n_chip)),
                dma((n_col,)), dma((n_col,)),
                dma((5,)),
            ],
            compiler_params=pltpu.CompilerParams(
                collective_id=0, has_side_effects=True, vmem_limit_bytes=62 * 2**20
            ),
            cost_estimate=pl.CostEstimate(
                flops=2 * rows * width * (total + d_cols * n_col),
                bytes_accessed=2 * total * (rows + width),
                transcendentals=0,
            ),
        )(amplitudes, integrals, dressing)
    )


def solution(mesh):
    placed = (P("row", "col"), P("row", "col"), P(None, "col"))
    return jax.shard_map(
        functools.partial(per_device, mesh.shape["row"], mesh.shape["col"]),
        mesh=mesh,
        in_specs=placed,
        out_specs=(P("row", "col"), P("row", "col")),
        check_vma=False,
    )
```

time: 577 us -> 329 us (0.57)
  waiting for transfers between devices: 463 us -> 0 us
  Pallas kernels: 0 us -> 322 us
  blocking collectives: 58.2 us -> 0 us
  matrix products: 35.6 us -> 0 us
  between operations: 13.8 us -> 0.65 us
    all_gather x3 -> x0, waiting for transfers between devices: 337 us -> none  [the longest x1 168 us: per_device(): amp_rows = lax.all_gather(amplitudes, 'col', axis=1, tiled=True)]
    pallas_call x0 -> x1, Pallas kernels: none -> 322 us  [per_device(): pl.pallas_call(functools.partial(kernel, n_row, n_col, part), out_shape=[...]
    reduce_scatter x1 -> x0, waiting for transfers between devices: 125 us -> none  [per_device(): lax.psum_scatter(lax.dot_general(rounded, wide_rows, (((0,), (0,)), ((),...]
    all_to_all x1 -> x0, blocking collectives: 58.2 us -> none  [per_device(): lax.all_to_all(summed, 'col', split_axis=1, concat_axis=0, tiled=True)]
    dot_general x2 -> x0, matrix products: 35.6 us -> none  [the longest x1 21 us: per_device(): jnp.dot(amp_rows, lax.all_gather(integrals, 'row', axis=0, tiled=True), p...]
  transfers between devices with their start and end apart: 4 -> 0, of which waited for: 4 -> 0; matrix products, arithmetic and copies ran while one was open for 4% -> 0% of each run, Pallas kernels for 0% -> 0%
where the time goes in v1:
time: 329 us
  Pallas kernels  322 us (98%)
  local copies, waits for them, and re-layouts  6.4 us (2%)
    pallas_call x1, Pallas kernels, per_device(): pl.pallas_call(functools.partial(kernel, n_row, n_col, part), out_shape=[...  322 us

profile of v1, /device:TPU:0, one launch (start us, length us, event | category | flops | bytes accessed | tf_op | source)
XLA Modules:
  0.0 329.1 jit_solution(16109089242063706134)
XLA Ops:
  0.6 322.1 %shard_map.50 = (f32[768,1536]{1,0:T(8,128)}, f32[768,768]{1,0:T(8,128)}) custom-call(bf16[768,1536]{1,0:T(8,128)(2,1)} %a_ref.1, bf16[768,1536]{1,0:T(8,128)(2,1)} %b_ref.1, bf16[6144,768]{1,0:T(8,128)(2,1)} %d_ref.1), custom_call_target="tpu_custom_call" | custom-call | flops 21743271936 | bytes 28311552 | tf_op jit(solution)/shard_map/pallas_call | solution.py:271
  322.7 0.0 copy-start
  322.7 5.0 %copy.7 = f32[768,1536]{1,0:T(8,128)} copy(f32[768,1536]{1,0:T(8,128)} %get-tuple-element.4) | data formatting | bytes 9437184
  327.7 0.0 copy-done
  327.7 1.4 copy.8
Async XLA Ops:
  322.7 5.0 %copy-start = (f32[768,768]{1,0:T(8,128)S(1)}, f32[768,768]{1,0:T(8,128)}, u32[]{:S(2)}) copy-start(f32[768,768]{1,0:T(8,128)} %get-tuple-element.5) | copy-start | bytes 7077892

commit v2 on v1

--- a/solution.py
+++ b/solution.py
@@ -18,9 +18,9 @@
 def kernel(
     n_row, n_col, part,
     a_ref, b_ref, d_ref, c_ref, out_ref,
-    abuf, bbuf, dbuf, acc, turned, mine, chipsum, others,
+    abuf, bbuf, dbuf, acc, turned, mine, chipsum, sent, others, landed,
     a_send, a_recv, d_send, d_recv, b_send, b_recv, s_send, s_recv,
-    x_send, x_recv, r_send, r_recv, o_send, o_recv, local,
+    x_send, x_recv, r_send, r_recv, o_send, o_recv, stored, local,
 ):
     n_chip = n_row // 2
     r, q = lax.axis_index("row"), lax.axis_index("col")
@@ -126,13 +126,17 @@
     for load in loads:
         load.wait()
 
-    middle = n_col // 2 + 1
-
-    @pl.loop(1, middle)
+    at_end = (q == 0) | (q == n_col - 1)
+    early = jnp.where(at_end, n_col // 2 + 1, n_col)
+
+    @pl.loop(1, early)
     def _(i):
         line_forward(*a_line, order(i))
 
-    line_start(*d_line)
+    @pl.when(at_end)
+    def _():
+        line_start(*d_line)
+
     for k in range(1, n_chip):
         b_arrival(k).wait_recv()
         s_copy(k).start()
@@ -152,11 +156,15 @@
 
     @pl.loop(0, n_col)
     def _(i):
-        @pl.when(i >= middle)
+        @pl.when(i >= early)
         def _():
             line_forward(*a_line, order(i))
 
         multiply(order(i))
+
+    @pl.when(jnp.logical_not(at_end))
+    def _():
+        line_start(*d_line)
 
     first_out = pltpu.make_async_copy(acc, c_ref, local.at[3])
     first_out.start()
@@ -171,38 +179,42 @@
         return remote(mine.at[1 - core], chipsum.at[z], x_send.at[z], x_recv.at[z], {"row": sibling})
 
     def r_copy(z, k):
-        target = lax.rem(chip + k, n_chip)
         return remote(
-            chipsum.at[z, target], others.at[z, k - 1], r_send.at[z, k], r_recv.at[z, k], {"row": peer(k)}
+            sent.at[z, k - 1], others.at[z, k - 1], r_send.at[z, k], r_recv.at[z, k], {"row": peer(k)}
         )
 
-    def o_copy(z, sem):
-        place = out_ref.at[pl.ds(pl.multiple_of(q * part, part), part), :]
-        return remote(chipsum.at[z, chip], place, o_send.at[z], o_recv.at[sem], {"col": z})
+    def o_copy(z):
+        return remote(others.at[z, 0], landed.at[q], o_send.at[z], o_recv.at[q], {"col": z})
 
     def o_arrival(z):
+        return remote(landed.at[z], landed.at[z], o_send.at[z], o_recv.at[z], {"col": z})
+
+    def o_store(z):
         place = out_ref.at[pl.ds(pl.multiple_of(z * part, part), part), :]
-        return remote(place, place, o_send.at[z], o_recv.at[z], {"col": z})
-
-    def o_own():
-        place = out_ref.at[pl.ds(pl.multiple_of(q * part, part), part), :]
-        return pltpu.make_async_copy(chipsum.at[q, chip], place, local.at[4])
+        return pltpu.make_async_copy(chipsum.at[z, chip], place, stored.at[z])
+
+    def held(z):
+        return (z != q) & jnp.logical_not(at_end) & ((z == 0) | (z == n_col - 1))
 
     def finish(z):
         for k in range(1, n_chip):
             r_copy(z, k).wait_recv()
         total = chipsum[z, chip]
         for k in range(1, n_chip):
-            total += others[z, k - 1]
-        chipsum[z, chip] = total
+            total += others[z, k - 1].astype(F32)
 
         @pl.when(z == q)
         def _():
-            o_own().start()
+            chipsum[z, chip] = total
+            o_store(z).start()
 
         @pl.when(z != q)
         def _():
-            o_copy(z, q).start()
+            others[z, 0] = total.astype(others.dtype)
+
+        @pl.when((z != q) & jnp.logical_not(held(z)))
+        def _():
+            o_copy(z).start()
 
     @pl.loop(0, n_col)
     def _(i):
@@ -229,17 +241,25 @@
             finish(order(i - 1))
 
         x_copy(z).wait_recv()
-        for k in range(n_chip):
-            chipsum[z, k] += mine[core, k]
         for k in range(1, n_chip):
+            target = lax.rem(chip + k, n_chip)
+            sent[z, k - 1] = (chipsum[z, target] + mine[core, target]).astype(sent.dtype)
             r_copy(z, k).start()
+        chipsum[z, chip] += mine[core, chip]
 
     last = order(jnp.int32(n_col - 1))
     finish(last)
 
     x_copy(last).wait_send()
+    line_drain(*d_line)
+
+    @pl.loop(0, n_col)
+    def _(z):
+        @pl.when(held(z))
+        def _():
+            o_copy(z).start()
+
     line_drain(*a_line)
-    line_drain(*d_line)
     for k in range(1, n_chip):
         b_copy(k).wait_send()
     for k in range(n_chip):
@@ -250,12 +270,21 @@
         for k in range(1, n_chip):
             r_copy(z, k).wait_send()
 
+    @pl.loop(1, n_col)
+    def _(i):
+        z = order(i)
+        o_arrival(z).wait_recv()
+        chipsum[z, chip] = landed[z].astype(F32)
+        o_store(z).start()
+
+    @pl.loop(0, n_col)
+    def _(z):
+        o_store(z).wait()
+
         @pl.when(z != q)
         def _():
-            o_copy(z, q).wait_send()
-            o_arrival(z).wait_recv()
-
-    o_own().wait()
+            o_copy(z).wait_send()
+
     first_out.wait()
 
 
@@ -284,13 +313,15 @@
                 pltpu.VMEM((width, rows), bf16),
                 pltpu.VMEM((2, n_chip, part, d_cols), F32),
                 pltpu.VMEM((n_col, n_chip, part, d_cols), F32),
-                pltpu.VMEM((n_col, n_chip - 1, part, d_cols), F32),
+                pltpu.VMEM((n_col, n_chip - 1, part, d_cols), bf16),
+                pltpu.VMEM((n_col, n_chip - 1, part, d_cols), bf16),
+                pltpu.VMEM((n_col, part, d_cols), bf16),
                 dma((n_col, 2)), dma((n_col,)), dma((n_col, 2)), dma((n_col,)),
                 dma((n_chip,)), dma((n_chip,)), dma((n_chip,)), dma((n_chip,)),
                 dma((n_col,)), dma((n_col,)),
                 dma((n_col, n_chip)), dma((n_col, n_chip)),
-                dma((n_col,)), dma((n_col,)),
-                dma((5,)),
+                dma((n_col,)), dma((n_col,)), dma((n_col,)),
+                dma((4,)),
             ],
             compiler_params=pltpu.CompilerParams(
                 collective_id=0, has_side_effects=True, vmem_limit_bytes=62 * 2**20

time: 329 us -> 276 us (0.84)
  Pallas kernels: 322 us -> 269 us
    pallas_call x1, Pallas kernels: 322 us -> 269 us  [per_device(): pl.pallas_call(functools.partial(kernel, n_row, n_col, part), out_shape=[...]
where the time goes in v2:
time: 276 us
  Pallas kernels  269 us (97%)
  local copies, waits for them, and re-layouts  6.4 us (2%)
    pallas_call x1, Pallas kernels, per_device(): pl.pallas_call(functools.partial(kernel, n_row, n_col, part), out_shape=[...  269 us
    unnamed x4, local copies, waits for them, and re-layouts  6.4 us

profile of v2, /device:TPU:0, one launch (start us, length us, event | category | flops | bytes accessed | tf_op | source)
XLA Modules:
  0.0 276.3 jit_solution(16469177623495355671)
XLA Ops:
  0.6 269.3 %shard_map.50 = (f32[768,1536]{1,0:T(8,128)}, f32[768,768]{1,0:T(8,128)}) custom-call(bf16[768,1536]{1,0:T(8,128)(2,1)} %a_ref.1, bf16[768,1536]{1,0:T(8,128)(2,1)} %b_ref.1, bf16[6144,768]{1,0:T(8,128)(2,1)} %d_ref.1), custom_call_target="tpu_custom_call" | custom-call | flops 21743271936 | bytes 28311552 | tf_op jit(solution)/shard_map/pallas_call | solution.py:300
  269.9 0.0 copy-start
  269.9 5.0 %copy.7 = f32[768,1536]{1,0:T(8,128)} copy(f32[768,1536]{1,0:T(8,128)} %get-tuple-element.4) | data formatting | bytes 9437184
  274.9 0.0 copy-done
  274.9 1.4 copy.8
Async XLA Ops:
  269.9 5.0 %copy-start = (f32[768,768]{1,0:T(8,128)S(1)}, f32[768,768]{1,0:T(8,128)}, u32[]{:S(2)}) copy-start(f32[768,768]{1,0:T(8,128)} %get-tuple-element.5) | copy-start | bytes 7077892

commit v3 on v2

v3 whole, which is shorter than its diff:
```python
import functools

import jax
import jax.numpy as jnp
from jax import lax
from jax.experimental import pallas as pl
from jax.experimental.pallas import tpu as pltpu
from jax.sharding import PartitionSpec as P

MESH = pl.DeviceIdType.MESH
F32 = jnp.float32


def tile_of(size, largest):
    return max(t for t in range(128, largest + 1, 128) if size % t == 0)


def kernel(
    n_row, n_col, part,
    a_ref, b_ref, d_ref, c_ref, out_ref,
    abuf, bbuf, dbuf, acc, turned, mine, chipsum, sent, others, landed,
    a_send, a_recv, d_send, d_recv, b_send, b_recv, s_send, s_recv,
    x_send, x_recv, r_send, r_recv, o_send, o_recv, stored, loaded_a, loaded_d, loaded_b,
):
    n_chip = n_row // 2
    r, q = lax.axis_index("row"), lax.axis_index("col")
    core, chip = lax.rem(r, 2), lax.div(r, 2)
    sibling = r + 1 - 2 * core
    a_rows, depth = a_ref.shape
    b_rows, width = b_ref.shape
    d_cols = dbuf.shape[2]
    a_cut, d_cut = abuf.shape[0] // n_col, dbuf.shape[0] // n_col
    piece = abuf.shape[2]

    def peer(dist):
        return lax.rem(chip + dist, n_chip) * 2 + core

    def order(i):
        room = jnp.minimum(q, n_col - 1 - q)
        half = lax.div(i + 1, 2)
        near = jnp.where(lax.rem(i, 2) == 1, q - half, q + half)
        far = jnp.where(q <= n_col - 1 - q, i, n_col - 1 - i)
        return jnp.where(i <= 2 * room, near, far)

    def remote(src, dst, send, recv, where):
        return pltpu.make_async_remote_copy(
            src_ref=src, dst_ref=dst, send_sem=send, recv_sem=recv, device_id=where, device_id_type=MESH
        )

    barrier = pltpu.get_barrier_semaphore()
    partners = [{"row": peer(k)} for k in range(1, n_chip)] + [{"row": sibling}]
    partners += [{"col": lax.rem(q + k, n_col)} for k in range(1, n_col)]
    for where in partners:
        pl.semaphore_signal(barrier, inc=1, device_id=where, device_id_type=MESH)
    pl.semaphore_wait(barrier, len(partners))

    def b_slot(owner):
        return bbuf.at[pl.ds(pl.multiple_of(owner * b_rows, b_rows), b_rows), :]

    def b_copy(k):
        return remote(b_ref, b_slot(r), b_send.at[k], b_recv.at[k], {"row": peer(k)})

    def b_arrival(k):
        slot = b_slot(peer(n_chip - k))
        return remote(slot, slot, b_send.at[k], b_recv.at[k], {"row": peer(k)})

    def s_copy(k):
        slot = b_slot(peer(n_chip - k))
        src = b_ref if k == 0 else slot
        return remote(src, slot, s_send.at[k], s_recv.at[k], {"row": sibling})

    def s_arrival(k):
        slot = b_slot(lax.rem(chip + n_chip - k, n_chip) * 2 + 1 - core)
        return remote(slot, slot, s_send.at[k], s_recv.at[k], {"row": sibling})

    def own_a(h):
        return a_ref.at[:, pl.ds(h * piece, piece)]

    def own_d(h):
        rows = pl.ds(pl.multiple_of(r * a_rows, a_rows), a_rows)
        return d_ref.at[rows, pl.ds(h * d_cols, d_cols)]

    def line_copy(buf, send, recv, cut, slot, side, src=None):
        src = buf.at[slot] if src is None else src
        return remote(src, buf.at[slot], send.at[slot, side], recv.at[slot], {"col": q - 1 + 2 * side})

    def line_start(own, buf, send, recv, cut):
        for h in range(cut):

            @pl.when(q > 0)
            def _():
                line_copy(buf, send, recv, cut, q * cut + h, 0, own(h)).start()

            @pl.when(q < n_col - 1)
            def _():
                line_copy(buf, send, recv, cut, q * cut + h, 1, own(h)).start()

    def line_forward(own, buf, send, recv, cut, z, h):
        slot = z * cut + h
        line_copy(buf, send, recv, cut, slot, jnp.where(z < q, 0, 1)).wait_recv()

        @pl.when((z < q) & (q < n_col - 1))
        def _():
            line_copy(buf, send, recv, cut, slot, 1).start()

        @pl.when((z > q) & (q > 0))
        def _():
            line_copy(buf, send, recv, cut, slot, 0).start()

    def line_drain(own, buf, send, recv, cut):
        @pl.loop(0, n_col)
        def _(z):
            for h in range(cut):

                @pl.when((z <= q) & (q < n_col - 1))
                def _():
                    line_copy(buf, send, recv, cut, z * cut + h, 1).wait_send()

                @pl.when((z >= q) & (q > 0))
                def _():
                    line_copy(buf, send, recv, cut, z * cut + h, 0).wait_send()

    a_line = (own_a, abuf, a_send, a_recv, a_cut)
    d_line = (own_d, dbuf, d_send, d_recv, d_cut)

    line_start(*a_line)
    for k in range(1, n_chip):
        b_copy(k).start()
    s_copy(0).start()
    loads = [pltpu.make_async_copy(b_ref, b_slot(r), loaded_b.at[0])]
    for h in range(a_cut):
        loads.append(pltpu.make_async_copy(own_a(h), abuf.at[q * a_cut + h], loaded_a.at[h]))
    for h in range(d_cut):
        loads.append(pltpu.make_async_copy(own_d(h), dbuf.at[q * d_cut + h], loaded_d.at[h]))
    for load in loads:
        load.start()
    for load in loads:
        load.wait()

    at_end = (q == 0) | (q == n_col - 1)
    early = jnp.where(at_end, n_col // 2 + 1, n_col)

    @pl.loop(1, early)
    def _(away):
        for h in range(a_cut):
            for z in (q - away, q + away):

                @pl.when((z >= 0) & (z < n_col))
                def _():
                    line_forward(*a_line, z, h)

    @pl.when(at_end)
    def _():
        line_start(*d_line)

    for k in range(1, n_chip):
        b_arrival(k).wait_recv()
        s_copy(k).start()

    def multiply(slot):
        tile = tile_of(width, 256)

        @pl.loop(0, width // tile)
        def _(j):
            cols = pl.ds(pl.multiple_of(j * tile, tile), tile)
            rows = pl.ds(pl.multiple_of(slot * piece, piece), piece)
            acc[:, cols] += jnp.dot(abuf[slot], bbuf[rows, cols], preferred_element_type=F32)

    acc[...] = jnp.zeros_like(acc)
    for k in range(n_chip):
        s_arrival(k).wait_recv()

    @pl.loop(0, n_col)
    def _(i):
        for h in range(a_cut):

            @pl.when(i >= early)
            def _():
                line_forward(*a_line, order(i), h)

            multiply(order(i) * a_cut + h)

    @pl.when(jnp.logical_not(at_end))
    def _():
        line_start(*d_line)

    first_out = pltpu.make_async_copy(acc, c_ref, loaded_b.at[1])
    first_out.start()
    turn = tile_of(width, 256)

    @pl.loop(0, width // turn)
    def _(j):
        at = pl.ds(pl.multiple_of(j * turn, turn), turn)
        turned[at, :] = acc[:, at].T.astype(turned.dtype)

    def x_copy(z):
        return remote(mine.at[1 - core], chipsum.at[z], x_send.at[z], x_recv.at[z], {"row": sibling})

    def r_copy(z, k):
        return remote(
            sent.at[z, k - 1], others.at[z, k - 1], r_send.at[z, k], r_recv.at[z, k], {"row": peer(k)}
        )

    def line_of(slot):
        return lax.div(slot, d_cut)

    def half_of(slot):
        return lax.rem(slot, d_cut)

    def slot_at(i):
        return order(lax.div(i, d_cut)) * d_cut + lax.rem(i, d_cut)

    def o_copy(slot):
        mark = q * d_cut + half_of(slot)
        return remote(others.at[slot, 0], landed.at[mark], o_send.at[slot], o_recv.at[mark], {"col": line_of(slot)})

    def o_arrival(slot):
        return remote(landed.at[slot], landed.at[slot], o_send.at[slot], o_recv.at[slot], {"col": line_of(slot)})

    def o_store(slot):
        rows = pl.ds(pl.multiple_of(line_of(slot) * part, part), part)
        cols = pl.ds(pl.multiple_of(half_of(slot) * d_cols, d_cols), d_cols)
        return pltpu.make_async_copy(chipsum.at[slot, chip], out_ref.at[rows, cols], stored.at[slot])

    def elsewhere(slot):
        return line_of(slot) != q

    def held(slot):
        z = line_of(slot)
        return (z != q) & jnp.logical_not(at_end) & ((z == 0) | (z == n_col - 1))

    def finish(z):
        for k in range(1, n_chip):
            r_copy(z, k).wait_recv()
        total = chipsum[z, chip]
        for k in range(1, n_chip):
            total += others[z, k - 1].astype(F32)

        @pl.when(jnp.logical_not(elsewhere(z)))
        def _():
            chipsum[z, chip] = total
            o_store(z).start()

        @pl.when(elsewhere(z))
        def _():
            others[z, 0] = total.astype(others.dtype)

        @pl.when(elsewhere(z) & jnp.logical_not(held(z)))
        def _():
            o_copy(z).start()

    @pl.loop(0, n_col * d_cut)
    def _(i):
        z = slot_at(i)

        @pl.when(i >= d_cut)
        def _():
            line_forward(*d_line, line_of(z), half_of(z))

        @pl.when(i > 0)
        def _():
            x_copy(slot_at(i - 1)).wait_send()

        tile = tile_of(d_cols, 384)

        @pl.loop(0, d_cols // tile)
        def _(j):
            cols = pl.ds(pl.multiple_of(j * tile, tile), tile)
            product = jnp.dot(turned[...], dbuf[z, :, cols], preferred_element_type=F32)
            for owner in range(n_row):
                mine[owner % 2, owner // 2, :, cols] = product[owner * part : (owner + 1) * part]

        x_copy(z).start()

        @pl.when(i > 0)
        def _():
            finish(slot_at(i - 1))

        x_copy(z).wait_recv()
        for k in range(1, n_chip):
            target = lax.rem(chip + k, n_chip)
            sent[z, k - 1] = (chipsum[z, target] + mine[core, target]).astype(sent.dtype)
            r_copy(z, k).start()
        chipsum[z, chip] += mine[core, chip]

    last = slot_at(jnp.int32(n_col * d_cut - 1))
    finish(last)

    x_copy(last).wait_send()
    line_drain(*d_line)

    @pl.loop(0, n_col * d_cut)
    def _(z):
        @pl.when(held(z))
        def _():
            o_copy(z).start()

    line_drain(*a_line)
    for k in range(1, n_chip):
        b_copy(k).wait_send()
    for k in range(n_chip):
        s_copy(k).wait_send()

    @pl.loop(0, n_col * d_cut)
    def _(z):
        for k in range(1, n_chip):
            r_copy(z, k).wait_send()

    @pl.loop(d_cut, n_col * d_cut)
    def _(i):
        z = slot_at(i)
        o_arrival(z).wait_recv()
        chipsum[z, chip] = landed[z].astype(F32)
        o_store(z).start()

    @pl.loop(0, n_col * d_cut)
    def _(z):
        o_store(z).wait()

        @pl.when(elsewhere(z))
        def _():
            o_copy(z).wait_send()

    first_out.wait()


def per_device(n_row, n_col, amplitudes, integrals, dressing):
    rows, depth = amplitudes.shape
    width, d_cols = integrals.shape[1], dressing.shape[1]
    part, n_chip = width // n_row, n_row // 2
    bf16 = amplitudes.dtype
    dma = pltpu.SemaphoreType.DMA
    anywhere = pl.BlockSpec(memory_space=pl.ANY)
    total = depth * n_col
    a_cut = 2 if depth % 256 == 0 else 1
    d_cut = 2 if d_cols % 256 == 0 else 1
    d_piece, d_slots = d_cols // d_cut, n_col * d_cut
    return tuple(
        pl.pallas_call(
            functools.partial(kernel, n_row, n_col, part),
            out_shape=[
                jax.ShapeDtypeStruct((rows, width), F32),
                jax.ShapeDtypeStruct((part * n_col, d_cols), F32),
            ],
            in_specs=[anywhere] * 3,
            out_specs=[anywhere] * 2,
            scratch_shapes=[
                pltpu.VMEM((n_col * a_cut, rows, depth // a_cut), bf16),
                pltpu.VMEM((total, width), bf16),
                pltpu.VMEM((d_slots, rows, d_piece), bf16),
                pltpu.VMEM((rows, width), F32),
                pltpu.VMEM((width, rows), bf16),
                pltpu.VMEM((2, n_chip, part, d_piece), F32),
                pltpu.VMEM((d_slots, n_chip, part, d_piece), F32),
                pltpu.VMEM((d_slots, n_chip - 1, part, d_piece), bf16),
                pltpu.VMEM((d_slots, n_chip - 1, part, d_piece), bf16),
                pltpu.VMEM((d_slots, part, d_piece), bf16),
                dma((n_col * a_cut, 2)), dma((n_col * a_cut,)), dma((d_slots, 2)), dma((d_slots,)),
                dma((n_chip,)), dma((n_chip,)), dma((n_chip,)), dma((n_chip,)),
                dma((d_slots,)), dma((d_slots,)),
                dma((d_slots, n_chip)), dma((d_slots, n_chip)),
                dma((d_slots,)), dma((d_slots,)), dma((d_slots,)),
                dma((a_cut,)), dma((d_cut,)), dma((2,)),
            ],
            compiler_params=pltpu.CompilerParams(
                collective_id=0, has_side_effects=True, vmem_limit_bytes=62 * 2**20
            ),
            cost_estimate=pl.CostEstimate(
                flops=2 * rows * width * (total + d_cols * n_col),
                bytes_accessed=2 * total * (rows + width),
                transcendentals=0,
            ),
        )(amplitudes, integrals, dressing)
    )


def solution(mesh):
    placed = (P("row", "col"), P("row", "col"), P(None, "col"))
    return jax.shard_map(
        functools.partial(per_device, mesh.shape["row"], mesh.shape["col"]),
        mesh=mesh,
        in_specs=placed,
        out_specs=(P("row", "col"), P("row", "col")),
        check_vma=False,
    )
```

time: 276 us -> 266 us (0.964)
  Pallas kernels: 269 us -> 258 us
    pallas_call x1, Pallas kernels: 269 us -> 258 us  [per_device(): pl.pallas_call(functools.partial(kernel, n_row, n_col, part), out_shape=[...]
where the time goes in v3:
time: 266 us; the launch traced here: 265 us
  Pallas kernels  258 us (97%)
  local copies, waits for them, and re-layouts  6.4 us (2%)
    pallas_call x1, Pallas kernels, per_device(): pl.pallas_call(functools.partial(kernel, n_row, n_col, part), out_shape=[...  258 us
    unnamed x4, local copies, waits for them, and re-layouts  6.4 us

profile of v3, /device:TPU:0, one launch (start us, length us, event | category | flops | bytes accessed | tf_op | source)
XLA Modules:
  0.0 264.7 jit_solution(10956351719761937053)
XLA Ops:
  0.6 257.7 %shard_map.50 = (f32[768,1536]{1,0:T(8,128)}, f32[768,768]{1,0:T(8,128)}) custom-call(bf16[768,1536]{1,0:T(8,128)(2,1)} %a_ref.1, bf16[768,1536]{1,0:T(8,128)(2,1)} %b_ref.1, bf16[6144,768]{1,0:T(8,128)(2,1)} %d_ref.1), custom_call_target="tpu_custom_call" | custom-call | flops 21743271936 | bytes 28311552 | tf_op jit(solution)/shard_map/pallas_call | solution.py:339
  258.3 0.0 copy-start
  258.3 5.0 %copy.7 = f32[768,1536]{1,0:T(8,128)} copy(f32[768,1536]{1,0:T(8,128)} %get-tuple-element.4) | data formatting | bytes 9437184
  263.3 0.0 copy-done
  263.3 1.4 copy.8
Async XLA Ops:
  258.3 5.0 %copy-start = (f32[768,768]{1,0:T(8,128)S(1)}, f32[768,768]{1,0:T(8,128)}, u32[]{:S(2)}) copy-start(f32[768,768]{1,0:T(8,128)} %get-tuple-element.5) | copy-start | bytes 7077892
